TPU v7x, 256 devices: a whole 4x4x8 slice. The times are simulated.
256 devices in a mesh: space: 16 (over y_lo, z), vel: 16 (over y_hi, x, core).
Axes of the slice: x: 4, y: 4 (y_hi: 2, y_lo: 2; y = y_hi * 2 + y_lo), z: 8, core: 2. Of those that a mesh axis runs over, the one named last changes fastest.
Arguments:
- dist: float32 [192, 4, 4, 32768], P('space', None, None, 'vel'), may hold values from 0.2 to 5
- cell_kind: int32 [192, 4, 4], P('space'), may hold values from 0 to 2
- inflow: float32 [32768], P('vel'), may hold values from 0.2 to 5
- wall_shape: float32 [32768], P('vel'), may hold values from 0.2 to 5
- gain_tables: float32 [1, 32768], replicated, may hold values from -6 to 6
- second_tables: float32 [1, 32768], replicated, may hold values from -6 to 6
Outputs:
- advanced: float32 [192, 4, 4, 32768], P('space', None, None, 'vel')
Inputs may be any that keep to these rules, and one draw needn't show every extreme that they name: `cell_kind`: 0 marks a gas cell, 1 a wall cell, 2 an inflow cell.
All inputs are finite; a program needn't handle non-finite values.
Results may differ from a plain program's by a relative error of at most 0.0003.
Values sent between devices are 32-bit elements; how exact they have to be, the bound alone decides.
A program may use at most 192 MiB of HBM per device.

v0:
```python
import math

import jax
import jax.numpy as jnp
from jax import lax
from jax.sharding import PartitionSpec as P

VR = 32


CFL = 0.3
COLLISION_AXIS = 0.25
HIGH = lax.Precision.HIGHEST


def padded(cells, sides, width):
    for axis, dim in sides:
        count = lax.axis_size(axis)
        ends = count - 1
        head = lax.slice_in_dim(cells, 0, width, axis=dim)
        tail = lax.slice_in_dim(cells, cells.shape[dim] - width, cells.shape[dim], axis=dim)
        cells = jnp.concatenate(
            [
                lax.ppermute(tail, axis, [(i, (i + 1) % count) for i in range(ends)]),
                cells,
                lax.ppermute(head, axis, [((i + 1) % count, i) for i in range(ends)]),
            ],
            axis=dim,
        )
    return cells


def courant(index):
    first = index // (VR * VR)
    second = index // VR % VR
    third = index % VR
    return tuple(
        (
            CFL * (2 * part - (VR - 1)).astype(jnp.float32) / (VR - 1)
            for part in (first, second, third)
        )
    )


def minmod(left, right):
    return 0.5 * (jnp.sign(left) + jnp.sign(right)) * jnp.minimum(jnp.abs(left), jnp.abs(right))


def cropped_field(array, lower, upper, axis):
    return lax.slice_in_dim(array, lower, array.shape[axis] - upper, axis=axis)


def face_terms(ext, speed, axis):
    left = cropped_field(ext, 0, 2, axis)
    middle = cropped_field(ext, 1, 1, axis)
    right = cropped_field(ext, 2, 0, axis)
    slope = minmod(middle - left, right - middle)
    upper = jnp.maximum(speed, 0.0)
    lower = jnp.minimum(speed, 0.0)
    flux = upper * (
        cropped_field(middle, 0, 1, axis) + 0.5 * (1.0 - upper) * cropped_field(slope, 0, 1, axis)
    )
    flux = flux + lower * (
        cropped_field(middle, 1, 0, axis) - 0.5 * (1.0 + lower) * cropped_field(slope, 1, 0, axis)
    )
    return cropped_field(flux, 1, 0, axis) - cropped_field(flux, 0, 1, axis)


def advect_cells(ext, speeds):
    core = ext[2:-2]
    change = face_terms(ext, speeds[0], 0)
    ext_y = jnp.concatenate([core[:, -2:], core, core[:, :2]], 1)
    change = change + face_terms(ext_y, speeds[1], 1)
    ext_z = jnp.concatenate([core[:, :, -2:], core, core[:, :, :2]], 2)
    change = change + face_terms(ext_z, speeds[2], 2)
    return core - change


def boundary(dist, cell_kind, inflow, wall_shape, scale):
    kind = cell_kind[..., None]
    walls = scale[..., None] * wall_shape
    return jnp.where(kind == 2, inflow, jnp.where(kind == 1, walls, dist))


def line_tables():
    points = jnp.arange(VR, dtype=jnp.int32)
    product = points[:, None] * points[None, :] % VR
    angle = 2.0 * math.pi / VR * product.astype(jnp.float32)
    return (jnp.cos(angle), jnp.sin(angle))


def plane_tables():
    plane = jnp.arange(VR * VR, dtype=jnp.int32)
    outer = plane // VR
    inner = plane % VR
    product = (outer[:, None] * outer[None, :] + inner[:, None] * inner[None, :]) % VR
    angle = 2.0 * math.pi / VR * product.astype(jnp.float32)
    return (jnp.cos(angle), jnp.sin(angle))


def first_axis(spectrum_real, imag_part, cosine, sine, sign):
    cos_real = jnp.einsum("kj,njm->nkm", cosine, spectrum_real, precision=HIGH)
    cos_imag = jnp.einsum("kj,njm->nkm", cosine, imag_part, precision=HIGH)
    sin_real = jnp.einsum("kj,njm->nkm", sine, spectrum_real, precision=HIGH)
    sin_imag = jnp.einsum("kj,njm->nkm", sine, imag_part, precision=HIGH)
    return (cos_real + sign * sin_imag, cos_imag - sign * sin_real)


def plane_axes(spectrum_real, imag_part, cos_plane, sin_plane, sign):
    shape = spectrum_real.shape
    flat_real = spectrum_real.reshape(-1, shape[2])
    flat_imag = imag_part.reshape(-1, shape[2])
    cos_real = jnp.dot(flat_real, cos_plane, precision=HIGH)
    cos_imag = jnp.dot(flat_imag, cos_plane, precision=HIGH)
    sin_real = jnp.dot(flat_real, sin_plane, precision=HIGH)
    sin_imag = jnp.dot(flat_imag, sin_plane, precision=HIGH)
    return (
        (cos_real + sign * sin_imag).reshape(shape),
        (cos_imag - sign * sin_real).reshape(shape),
    )


def inverse(spectrum_real, imag_part, tables, total_v):
    cosine, sine, cos_plane, sin_plane = tables
    spectrum_real, imag_part = first_axis(spectrum_real, imag_part, cosine, sine, -1.0)
    spectrum_real, imag_part = plane_axes(spectrum_real, imag_part, cos_plane, sin_plane, -1.0)
    return (spectrum_real / total_v, imag_part / total_v)


def collide(cell_grid, gain_tables, second_tables):
    cell_count = cell_grid.shape[0]
    total_v = cell_grid.shape[1]
    cosine, sine = line_tables()
    cos_plane, sin_plane = plane_tables()
    tables = (cosine, sine, cos_plane, sin_plane)
    field = cell_grid.reshape(cell_count, VR, VR * VR)
    flat = field.reshape(-1, VR * VR)
    spec_real = jnp.dot(flat, cos_plane, precision=HIGH).reshape(field.shape)
    spec_imag = -jnp.dot(flat, sin_plane, precision=HIGH).reshape(field.shape)
    spec_real, spec_imag = first_axis(spec_real, spec_imag, cosine, sine, 1.0)
    weight_a = gain_tables[0].reshape(VR, VR * VR)
    second_weight = second_tables[0].reshape(VR, VR * VR)
    first_r, first_i = inverse(weight_a * spec_real, weight_a * spec_imag, tables, total_v)
    second_r, second_i = inverse(
        second_weight * spec_real, second_weight * spec_imag, tables, total_v
    )
    total_mass = first_r * second_r - first_i * second_i
    return cell_grid + COLLISION_AXIS * total_mass.reshape(cell_count, -1)


def shards(dist, cell_kind, inflow, wall_shape, gain_tables, second_tables):
    v_dev = dist.shape[3]
    groups = lax.axis_size("vel")
    total_v = v_dev * groups
    index = lax.axis_index("vel") * v_dev + jnp.arange(v_dev, dtype=jnp.int32)
    speeds = courant(index)
    mass, wall_mass = lax.psum((jnp.sum(dist, axis=3), jnp.sum(wall_shape)), "vel")
    rho = mass / total_v
    wall_mean = wall_mass / total_v
    start = boundary(dist, cell_kind, inflow, wall_shape, rho / wall_mean)
    ext = padded(start, (("space", 0),), 2)
    read = advect_cells(ext, speeds)
    number = read.shape[0] * read.shape[1] * read.shape[2]
    result = collide(
        lax.all_to_all(
            read.reshape(groups, number // groups, v_dev),
            "vel",
            split_axis=0,
            concat_axis=2,
            tiled=True,
        )[0],
        gain_tables,
        second_tables,
    )
    result = lax.all_to_all(result[None], "vel", split_axis=2, concat_axis=0, tiled=True)
    return result.reshape(read.shape)


def solution(mesh):
    placed = (P("space", None, None, "vel"), P("space", None, None), P("vel"), P("vel"), P(), P())
    return jax.shard_map(
        shards, mesh=mesh, in_specs=placed, out_specs=P("space", None, None, "vel"), check_vma=False
    )
```

profile of v0, /device:TPU:8, one launch (start us, length us, event | category | flops | bytes accessed | tf_op | source)
XLA Modules:
  0.0 674.6 jit_solution(17032740894748467637)
XLA Ops:
  4.1 68.7 %all-reduce = (f32[12,4,4]{2,1,0:T(4,128)S(1)}, f32[]{:T(128)}) all-reduce(f32[12,4,4]{2,1,0:T(4,128)S(1)} %reduce_sum.18, f32[]{:T(128)} %reduce_sum.19), channel_id=1, replica_groups=mesh['space'=16,'vel'=16] {'vel'}, use_global_device_ids=true, to_apply=%region_1.2 | all-reduce | flops 193 | bytes 1544 | tf_op jit(solution)/shard_map/psum | solution.py:157
  75.7 3.8 collective-permute-start
  79.5 6.6 collective-permute-start.1
  87.3 3.9 minimum_multiply_fusion.1
  91.2 4.1 minimum_multiply_fusion
  99.6 4.0 minimum_multiply_fusion.2
  103.6 2.5 fusion.50
  110.1 4.2 all-to-all-start
  116.9 26.7 %all-to-all-done = f32[16,12,2048]{2,1,0:T(8,128)S(1)} async-done(((f32[16,12,2048]{2,1,0:T(8,128)}), f32[16,12,2048]{2,1,0:T(8,128)S(1)}, u32[]{:S(2)}, u32[]{:S(2)}) %all-to-all-start) | async-done | bytes 1572896 | tf_op jit(solution)/shard_map/all_to_all | solution.py:165
  149.2 21.1 %fusion.3 = f32[12,32,1024]{2,1,0:T(8,128)S(1)} fusion(f32[12,32,1024]{2,1,0:T(8,128)S(1)} %dot_general.68, s32[1024]{0:T(1024)S(1)} %get-tuple-element.27, s32[1024]{0:T(1024)S(1)} %get-tuple-element.28), kind=kOutput, calls=%fused_computation.6 | convolution fusion | flops 4848615424 | bytes 3153920 | tf_op jit(solution)/shard_map/dot_general | solution.py:139
  170.3 21.9 %fusion.5 = f32[12,32,1024]{2,1,0:T(8,128)S(1)} fusion(f32[12,32,1024]{2,1,0:T(8,128)S(1)} %dot_general.68, s32[1024]{0:T(1024)S(1)} %get-tuple-element.27, s32[1024]{0:T(1024)S(1)} %get-tuple-element.28), kind=kOutput, calls=%fused_computation.8 | convolution fusion | flops 4848615424 | bytes 3153920 | tf_op jit(solution)/shard_map/dot_general | solution.py:138
  202.4 22.5 %fusion.20 = f32[384,1024]{1,0:T(8,128)} fusion(f32[384,1024]{1,0:T(8,128)S(1)} %bitcast.94, s32[1024]{0:T(1024)S(1)} %get-tuple-element.27, s32[1024]{0:T(1024)S(1)} %get-tuple-element.28), kind=kOutput, calls=%fused_computation.47 | convolution fusion | flops 4848615424 | bytes 3153920 | tf_op jit(solution)/shard_map/dot_general | solution.py:114
  224.9 22.5 %fusion.33 = f32[384,1024]{1,0:T(8,128)} fusion(f32[384,1024]{1,0:T(8,128)S(1)} %bitcast.95, s32[1024]{0:T(1024)S(1)} %get-tuple-element.27, s32[1024]{0:T(1024)S(1)} %get-tuple-element.28), kind=kOutput, calls=%fused_computation.53 | convolution fusion | flops 4848615424 | bytes 3153920 | tf_op jit(solution)/shard_map/dot_general | solution.py:116
  249.1 3.0 fusion.59
  255.6 22.7 %fusion.31 = f32[384,1024]{1,0:T(8,128)} fusion(f32[384,1024]{1,0:T(8,128)S(1)} %bitcast.96, s32[1024]{0:T(1024)S(1)} %get-tuple-element.27, s32[1024]{0:T(1024)S(1)} %get-tuple-element.28), kind=kOutput, calls=%fused_computation.52 | convolution fusion | flops 4848615424 | bytes 3153920 | tf_op jit(solution)/shard_map/dot_general | solution.py:115
  278.3 22.2 %fusion.26 = f32[384,1024]{1,0:T(8,128)} fusion(f32[384,1024]{1,0:T(8,128)S(1)} %bitcast.97, s32[1024]{0:T(1024)S(1)} %get-tuple-element.27, s32[1024]{0:T(1024)S(1)} %get-tuple-element.28), kind=kOutput, calls=%fused_computation.50 | convolution fusion | flops 4848615424 | bytes 3153920 | tf_op jit(solution)/shard_map/dot_general | solution.py:113
  302.3 22.5 %fusion.29 = f32[384,1024]{1,0:T(8,128)} fusion(f32[384,1024]{1,0:T(8,128)S(1)} %bitcast.92, s32[1024]{0:T(1024)S(1)} %get-tuple-element.27, s32[1024]{0:T(1024)S(1)} %get-tuple-element.28), kind=kOutput, calls=%fused_computation.51 | convolution fusion | flops 4848615424 | bytes 3153920 | tf_op jit(solution)/shard_map/dot_general | solution.py:115
  324.8 22.2 %fusion.24 = f32[384,1024]{1,0:T(8,128)} fusion(f32[384,1024]{1,0:T(8,128)S(1)} %bitcast.93, s32[1024]{0:T(1024)S(1)} %get-tuple-element.27, s32[1024]{0:T(1024)S(1)} %get-tuple-element.28), kind=kOutput, calls=%fused_computation.49 | convolution fusion | flops 4848615424 | bytes 3153920 | tf_op jit(solution)/shard_map/dot_general | solution.py:113
  347.1 3.0 squeeze.3
  350.1 3.1 multiply_subtract_fusion.1
  353.2 21.7 %fusion.22 = f32[384,1024]{1,0:T(8,128)S(1)} fusion(f32[384,1024]{1,0:T(8,128)S(1)} %bitcast.90, s32[1024]{0:T(1024)S(1)} %get-tuple-element.27, s32[1024]{0:T(1024)S(1)} %get-tuple-element.28), kind=kOutput, calls=%fused_computation.48 | convolution fusion | flops 4848615424 | bytes 3153920 | tf_op jit(solution)/shard_map/dot_general | solution.py:114
  375.0 23.0 %subtract_multiply_fusion = f32[384,1024]{1,0:T(8,128)S(1)} fusion(f32[384,1024]{1,0:T(8,128)S(1)} %copy-done.7, f32[384,1024]{1,0:T(8,128)S(1)} %copy-done.11, f32[384,1024]{1,0:T(8,128)S(1)} %fusion.22, f32[384,1024]{1,0:T(8,128)S(1)} %copy-done.9, f32[384,1024]{1,0:T(8,128)S(1)} %copy-done.12, f32[384,1024]{1,0:T(8,128)S(1)} %copy-done.8, ...), kind=kOutput, calls=%fused_computation.90 | convolution fusion | flops 4854906880 | bytes 14163968 | tf_op jit(solution)/shard_map/dot_general | solution.py:116
  398.1 3.0 mul.677
  401.1 3.0 add.385
  404.1 23.9 %copy.30 = f32[1,12,32768]{1,0,2:T(1,128)} copy(f32[1,12,32768]{2,0,1:T(1,128)S(1)} %add.385) | data formatting | bytes 3145728 | tf_op jit(solution)/shard_map/add | solution.py:148
  428.6 146.7 %reduce.8 = f32[32768,12]{1,0:T(8,128)} reduce(f32[32768,1,12]{2,1,0:T(1,128)} %bitcast.85, f32[]{:T(128)} %broadcast.974), dimensions={1}, to_apply=%bitcast.71.reduce_sub_computation | reduce | bytes 3145732
  575.3 18.2 %reshape.292 = f32[16,1,24576]{2,1,0:T(1,128)S(1)} reshape(f32[32768,12]{1,0:T(8,128)} %reduce.8) | data formatting | bytes 3145728
  593.5 28.2 %all_to_all.30 = f32[16,1,24576]{2,1,0:T(1,128)S(1)} all-to-all(f32[16,1,24576]{2,1,0:T(1,128)S(1)} %reshape.292), channel_id=1, replica_groups=mesh['space'=16,'vel'=16] {'vel'}, dimensions={0} | all-to-all | bytes 3145728 | tf_op jit(solution)/shard_map/all_to_all | solution.py:175
  621.8 4.4 reduce.9
  626.2 33.1 %reshape.293 = f32[32768,1,12]{2,1,0:T(1,128)} reshape(f32[16,24576]{1,0:T(8,128)S(1)} %reduce.9) | data formatting | bytes 3145728
  659.3 10.9 %copy.33 = f32[1,12,16,2048]{3,2,0,1:T(8,128)} copy(f32[1,12,16,2048]{1,3,2,0:T(8,128)} %bitcast.86) | data formatting | bytes 3145728 | tf_op jit(solution)/shard_map/all_to_all | solution.py:175
  670.2 2.3 copy.32
  (69 shorter events, 43.0 us)
Async XLA Ops:
  0.0 73.5 %copy-start = (f32[12,4,4,2048]{3,2,1,0:T(4,128)S(1)}, f32[12,4,4,2048]{3,2,1,0:T(4,128)}, u32[]{:S(2)}) copy-start(f32[12,4,4,2048]{3,2,1,0:T(4,128)} %param.6) | copy-start | bytes 4718596
  75.7 23.8 %collective-permute-start = (f32[2,4,4,2048]{3,2,1,0:T(4,128)}, f32[2,4,4,2048]{3,2,1,0:T(4,128)S(1)}, u32[]{:S(2)}, u32[]{:S(2)}) collective-permute-start(f32[2,4,4,2048]{3,2,1,0:T(4,128)} %get-tuple-element.7), channel_id=1, source_target_pairs={{0,16},{16,32},{32,48},{48,64},{64,80},{80,96},{96,112},{112,128},... | collective-permute-start | bytes 786440 | tf_op jit(solution)/shard_map/ppermute | solution.py:24
  79.5 20.0 %collective-permute-start.1 = (f32[2,4,4,2048]{3,2,1,0:T(4,128)}, f32[2,4,4,2048]{3,2,1,0:T(4,128)}, u32[]{:S(2)}, u32[]{:S(2)}) collective-permute-start(f32[2,4,4,2048]{3,2,1,0:T(4,128)} %get-tuple-element.8), channel_id=1, source_target_pairs={{16,0},{32,16},{48,32},{64,48},{80,64},{96,80},{112,96},{128,112},... | collective-permute-start | bytes 786440 | tf_op jit(solution)/shard_map/ppermute | solution.py:26
  103.6 2.6 copy-start.5
  103.6 2.6 copy-start.6
  110.1 4.7 copy-start.3
  110.1 5.7 copy-start.4
  110.1 33.4 %all-to-all-start = ((f32[16,12,2048]{2,1,0:T(8,128)}), f32[16,12,2048]{2,1,0:T(8,128)S(1)}, u32[]{:S(2)}, u32[]{:S(2)}) async-start(f32[16,12,2048]{2,1,0:T(8,128)} %reshape.266), calls=%async_computation | async-start | bytes 4194304 | tf_op jit(solution)/shard_map/all_to_all | solution.py:165
  324.8 22.2 %copy-start.1 = (f32[1,12,16,2048]{3,2,0,1:T(8,128)S(1)}, f32[1,12,16,2048]{3,2,0,1:T(8,128)}, u32[]{:S(2)}) copy-start(f32[1,12,16,2048]{3,2,0,1:T(8,128)} %copy.27) | copy-start | bytes 4718596
  353.2 21.8 %copy-start.7 = (f32[384,1024]{1,0:T(8,128)S(1)}, f32[384,1024]{1,0:T(8,128)}, u32[]{:S(2)}) copy-start(f32[384,1024]{1,0:T(8,128)} %fusion.20) | copy-start | bytes 4718596
  353.2 21.8 %copy-start.8 = (f32[384,1024]{1,0:T(8,128)S(1)}, f32[384,1024]{1,0:T(8,128)}, u32[]{:S(2)}) copy-start(f32[384,1024]{1,0:T(8,128)} %fusion.33) | copy-start | bytes 4718596
  353.2 21.8 %copy-start.9 = (f32[384,1024]{1,0:T(8,128)S(1)}, f32[384,1024]{1,0:T(8,128)}, u32[]{:S(2)}) copy-start(f32[384,1024]{1,0:T(8,128)} %fusion.31) | copy-start | bytes 4718596
  353.2 21.8 %copy-start.10 = (f32[384,1024]{1,0:T(8,128)S(1)}, f32[384,1024]{1,0:T(8,128)}, u32[]{:S(2)}) copy-start(f32[384,1024]{1,0:T(8,128)} %fusion.26) | copy-start | bytes 4718596
  353.2 21.8 %copy-start.11 = (f32[384,1024]{1,0:T(8,128)S(1)}, f32[384,1024]{1,0:T(8,128)}, u32[]{:S(2)}) copy-start(f32[384,1024]{1,0:T(8,128)} %fusion.29) | copy-start | bytes 4718596
  353.2 21.8 %copy-start.12 = (f32[384,1024]{1,0:T(8,128)S(1)}, f32[384,1024]{1,0:T(8,128)}, u32[]{:S(2)}) copy-start(f32[384,1024]{1,0:T(8,128)} %fusion.24) | copy-start | bytes 4718596
  398.0 3.0 copy-start.2
where the time goes:
time: 685 us; the launch traced here: 675 us
  matrix products  246 us (36%)
  other arithmetic  182 us (27%)
  local copies, waits for them, and re-layouts  107 us (16%)
  blocking collectives  97 us (14%)
  waiting for transfers between devices  26.7 us (4%)
  starting transfers between devices  14.7 us (2%)
    unnamed x3, other arithmetic  149 us
    psum x1, blocking collectives, shards(): lax.psum((jnp.sum(dist, axis=3), jnp.sum(wall_shape)), 'vel')  68.7 us
    unnamed x30, local copies, waits for them, and re-layouts  52.4 us
    dot_general x2, matrix products, plane_axes(): sin_imag = jnp.dot(flat_imag, sin_plane, precision=HIGH)  45.5 us
    dot_general x2, matrix products, plane_axes(): sin_real = jnp.dot(flat_real, sin_plane, precision=HIGH)  45.2 us
    dot_general x2, matrix products, plane_axes(): cos_real = jnp.dot(flat_real, cos_plane, precision=HIGH)  44.5 us
    dot_general x2, matrix products, plane_axes(): cos_imag = jnp.dot(flat_imag, cos_plane, precision=HIGH)  44.2 us
    all_to_all x1, blocking collectives, shards(): lax.all_to_all(result[None], 'vel', split_axis=2, concat_axis=0, tiled=True)  28.2 us
  transfers between devices with their start and end apart: 3, of which 1 were waited for; matrix products, arithmetic and copies ran while one was open for 2% of the time, Pallas kernels for 0%

commit v1 on v0

v1 whole, which is shorter than its diff:
```python
import functools
import math

import jax
import jax.numpy as jnp
import numpy as np
from jax import lax
from jax.experimental import pallas as pl
from jax.experimental.pallas import tpu as pltpu
from jax.sharding import PartitionSpec as P

VR = 32
NV = VR * VR * VR
CFL = 0.3
COLLISION_AXIS = 0.25
HIGH = lax.Precision.HIGHEST
MESH = pl.DeviceIdType.MESH
F32 = jnp.float32
BF16 = jnp.bfloat16

FULL = 136
HALF = 128
PAIR = 2

ORDER = (
    (1, 0, 0), (0, 1, 0), (0, 3, 1), (1, 2, 0), (1, 1, 0), (1, 3, 1), (0, 2, 0), (1, 0, 1),
    (0, 1, 1), (0, 3, 0), (1, 2, 1), (1, 1, 1), (1, 3, 0), (0, 2, 1), (0, 0, 1),
)


def halves(table):
    high = jnp.asarray(table, F32).astype(BF16)
    low = (jnp.asarray(table, F32) - high.astype(F32)).astype(BF16)
    return high, low


def np_halves(table):
    table = np.asarray(table, np.float32)
    high = table.astype(BF16)
    low = (table - high.astype(np.float32)).astype(BF16)
    return high, low


def tables():
    two_pi = 2.0 * math.pi
    row = np.arange(256)
    a, b_hi = row // 8, row % 8
    spec = np.arange(FULL)
    ka = np.where(spec < HALF, spec % 16, 16)
    r = np.where(spec < HALF, spec // 16, spec - HALF)
    theta = two_pi / 32 * ((ka[:, None] * a[None] + 4 * r[:, None] * b_hi[None]) % 32)
    left = np.concatenate([np.cos(theta), -np.sin(theta)], 0)
    lane = np.arange(128)
    b_lo, c = lane // 32, lane % 32
    angle = two_pi / 32 * ((8 * b_lo[:, None] * b_lo[None] + c[:, None] * c[None]) % 32)
    cos, sin = np.cos(angle), np.sin(angle)
    right = np.block([[cos, -sin], [sin, cos]])
    back = np.block([[cos, sin], [-sin, cos]])
    turn = two_pi / 32 * (r[:, None] * b_lo[None])
    twiddle = np.stack([np.cos(turn), np.sin(turn)])
    th = theta[:HALF].T
    phi = two_pi / 8 * ((r[None, :HALF] * b_hi[:, None]) % 8)
    sign = np.where(a % 2 == 0, 1.0, -1.0)[:, None]
    first = (ka[:HALF] == 0)[None]
    real = np.where(first, np.cos(phi) + sign * np.sin(phi), 2 * np.cos(th))
    imag = np.where(first, -np.sin(phi) + sign * np.cos(phi), -2 * np.sin(th))
    out = np.concatenate([real, imag], 1)
    source = ((-a) % 32) * 8
    flip0 = np.zeros((256, 256), np.float32)
    flip0[row, source + (-b_hi) % 8] = 1
    flip1 = np.zeros((256, 256), np.float32)
    flip1[row, source + (-b_hi - 1) % 8] = 1
    flip_lane = np.zeros((128, 128), np.float32)
    flip_lane[((-b_lo) % 4) * 32 + (-c) % 32, lane] = 1
    flips = np.concatenate([flip0, flip1], 0)
    mats = []
    for table in (left, right, back, out):
        mats += list(np_halves(table))
    return mats, twiddle.astype(np.float32), flips, flip_lane


def split(value):
    high = value.astype(BF16)
    return high, (value - high.astype(F32)).astype(BF16)


def mul3(left, right):
    dot = functools.partial(jnp.dot, preferred_element_type=F32)
    return dot(left[0], right[0]) + (dot(left[1], right[0]) + dot(left[0], right[1]))


def minmod(p, q):
    return jnp.maximum(jnp.minimum(p, q), jnp.minimum(jnp.maximum(p, q), 0.0))


def coords(vel):
    return vel // 8, (vel // 2) % 4, vel % 2


def partner(vel, off):
    y, x, core = coords(vel)
    return ((y + off[0]) % 2) * 8 + ((x + off[1]) % 4) * 2 + (core + off[2]) % 2


def step_kernel(
    spaces, layers,
    dist, kind, inflow, wall, gain, second, lh, ll, rh, rl, bh, bl, oh, ol, twiddle, flips, flip_lane,
    result,
    ext, lane_sums, mass_row, mass_all, scales, read, cells, done, nat, weights, weights16, yh, yl, vh, vl,
    in_sem, mass_send, mass_recv, halo_send, halo_recv, go_send, go_recv, back_send, back_recv, own_sem,
):
    sp = lax.axis_index("space")
    me = lax.axis_index("vel")
    my_y, my_z = me // 4, me % 4
    chunks = layers // PAIR
    count = layers * 16

    loads = []
    for l in range(16):
        loads.append(pltpu.make_async_copy(
            dist.at[:, :, :, pl.ds(128 * l, 128)],
            ext.at[pl.ds(2, layers), :, :, l, :],
            in_sem.at[l],
        ))
        loads[-1].start()

    barrier = pltpu.get_barrier_semaphore()
    for off in ORDER:
        pl.semaphore_signal(barrier, inc=1, device_id=(sp, partner(me, off)), device_id_type=MESH)
    for near in (1, spaces - 1):
        pl.semaphore_signal(barrier, inc=1, device_id=(lax.rem(sp + near, spaces), me), device_id_type=MESH)

    lane_sums[...] = jnp.zeros_like(lane_sums)
    lane_sums[count:count + 8, :] = jnp.concatenate(
        [jnp.sum(wall[...], axis=0, keepdims=True), jnp.zeros((7, 128), F32)], 0)
    for load in loads:
        load.wait()

    def sum_layer(x, _):
        block = ext[2 + x].reshape(16, 2, 8, 128)
        block = jnp.sum(block[:, 0] + block[:, 1], axis=1)
        lane_sums[pl.ds(pl.multiple_of(x * 16, 16), 16), :] = block
        return 0

    lax.fori_loop(0, layers, sum_layer, 0)
    mass_row[...] = jnp.sum(lane_sums[...].T, axis=0, keepdims=True)
    mass_all[me] = mass_row[...]

    pl.semaphore_wait(barrier, len(ORDER) + 2)

    sends = []
    for i, off in enumerate(ORDER):
        sends.append(pltpu.make_async_remote_copy(
            src_ref=mass_row, dst_ref=mass_all.at[me], send_sem=mass_send.at[i], recv_sem=mass_recv.at[i],
            device_id=(sp, partner(me, off)), device_id_type=MESH,
        ))
        sends[-1].start()

    lane = lax.broadcasted_iota(jnp.int32, (16, 128), 1) // 32
    sub = lax.broadcasted_iota(jnp.int32, (8, 128), 0)
    lane8 = lax.broadcasted_iota(jnp.int32, (8, 128), 1) // 32
    for t, (table, scale) in enumerate(((gain, 1.0 / NV), (second, COLLISION_AXIS / NV))):
        g = table[...]
        rev = jnp.dot(g, flip_lane[...], precision=HIGH, preferred_element_type=F32)
        mask = lax.broadcasted_iota(jnp.int32, (256, 128), 1) < 32
        rev0 = jnp.dot(flips[0:256, :], rev, precision=HIGH, preferred_element_type=F32)
        rev1 = jnp.dot(flips[256:512, :], rev, precision=HIGH, preferred_element_type=F32)
        rev = jnp.where(mask, rev0, rev1)
        nat[2 * t] = (0.5 * scale) * (g + rev)
        nat[2 * t + 1] = (0.5 * scale) * (g - rev)

    def order_weights(t, _):
        for r in range(8):
            high, low = r // 4, r % 4
            value = jnp.zeros((16, 128), F32)
            value16 = jnp.zeros((8, 128), F32)
            for q in range(4):
                rows = nat[t, pl.ds(2 * q + high, 16, stride=8), :]
                row16 = jnp.broadcast_to(nat[t, pl.ds(128 + 2 * q + high, 1), :], (8, 128))
                shift = (32 * (q - low)) % 128
                if shift:
                    rows = pltpu.roll(rows, shift, 1)
                    row16 = pltpu.roll(row16, shift, 1)
                value = jnp.where(lane == q, rows, value)
                value16 = jnp.where(lane8 == q, row16, value16)
            weights[t, 16 * r:16 * r + 16, :] = value
            weights16[t, 8 * r:8 * r + 8, :] = jnp.where(sub == 0, value16, 0.0)
        return 0

    lax.fori_loop(0, 4, order_weights, 0)

    for copy in sends:
        copy.wait()
    total = jnp.sum(mass_all[...], axis=0)
    totals = jnp.broadcast_to(total, (128, 256)).T
    scales[...] = totals[:count] / totals[count:count + 1]

    def boundary_layer(x, _):
        for y in range(4):
            for z in range(4):
                what = jnp.full((8, 128), kind[x, y, z], jnp.int32)
                scale = jnp.broadcast_to(scales[pl.ds(x * 16 + 4 * y + z, 1), :], (8, 128))
                for e in range(2):
                    rows = slice(8 * e, 8 * e + 8)
                    value = jnp.where(what == 1, scale * wall[rows, :], ext[2 + x, y, z, rows, :])
                    ext[2 + x, y, z, rows, :] = jnp.where(what == 2, inflow[rows, :], value)
        return 0

    lax.fori_loop(0, 2, boundary_layer, 0)
    lax.fori_loop(layers - 2, layers, boundary_layer, 0)
    to_left = pltpu.make_async_remote_copy(
        src_ref=ext.at[pl.ds(2, 2)], dst_ref=ext.at[pl.ds(layers + 2, 2)],
        send_sem=halo_send.at[0], recv_sem=halo_recv.at[0],
        device_id=(lax.rem(sp + spaces - 1, spaces), me), device_id_type=MESH)
    to_right = pltpu.make_async_remote_copy(
        src_ref=ext.at[pl.ds(layers, 2)], dst_ref=ext.at[pl.ds(0, 2)],
        send_sem=halo_send.at[1], recv_sem=halo_recv.at[1],
        device_id=(lax.rem(sp + 1, spaces), me), device_id_type=MESH)

    @pl.when(sp > 0)
    def _():
        to_left.start()

    @pl.when(sp < spaces - 1)
    def _():
        to_right.start()

    @pl.when(sp == 0)
    def _():
        ext[0:2] = jnp.zeros((2, 4, 4, 16, 128), F32)

    @pl.when(sp == spaces - 1)
    def _():
        ext[layers + 2:layers + 4] = jnp.zeros((2, 4, 4, 16, 128), F32)

    lax.fori_loop(2, layers - 2, boundary_layer, 0)

    b_index = 4 * lax.broadcasted_iota(jnp.int32, (8, 128), 0) + lane8
    c_index = lax.broadcasted_iota(jnp.int32, (8, 128), 1) % 32

    def speed(index):
        return CFL * (2 * index - (VR - 1)).astype(F32) / (VR - 1)

    nu_y, nu_z = speed(b_index), speed(c_index)
    up_y, up_z = nu_y > 0, nu_z > 0
    size_y, size_z = jnp.abs(nu_y), jnp.abs(nu_z)
    coef_y = jnp.where(up_y, 0.5, -0.5) * (1.0 - size_y)
    coef_z = jnp.where(up_z, 0.5, -0.5) * (1.0 - size_z)

    def ring(s, coef, up, size):
        diff = [s[(i + 1) % 4] - s[i] for i in range(4)]
        face = [s[i] + coef * minmod(diff[i - 1], diff[i]) for i in range(4)]
        step = [face[(i + 1) % 4] - face[i] for i in range(4)]
        return [size * jnp.where(up, step[i - 1], -step[i]) for i in range(4)]

    def transport(x0):
        for e in range(2):
            rows = slice(8 * e, 8 * e + 8)
            nu_x = speed(jnp.full((8, 128), 2 * me + e, jnp.int32))
            up_x = nu_x > 0
            size_x = jnp.abs(nu_x)
            coef_x = jnp.where(up_x, 0.5, -0.5) * (1.0 - size_x)
            for y in range(4):
                for z in range(4):
                    s = [ext[x0 + i, y, z, rows, :] for i in range(6)]
                    diff = [s[i + 1] - s[i] for i in range(5)]
                    face = [s[i + 1] + coef_x * minmod(diff[i], diff[i + 1]) for i in range(4)]
                    step = [face[i + 1] - face[i] for i in range(3)]
                    for i in range(PAIR):
                        read[x0 + i, 4 * y + z, rows, :] = s[i + 2] - size_x * jnp.where(up_x, step[i], -step[i + 1])
            for i in range(PAIR):
                s = [[ext[x0 + 2 + i, y, z, rows, :] for z in range(4)] for y in range(4)]
                along_z = [ring(s[y], coef_z, up_z, size_z) for y in range(4)]
                along_y = [ring([s[y][z] for y in range(4)], coef_y, up_y, size_y) for z in range(4)]
                for y in range(4):
                    for z in range(4):
                        read[x0 + i, 4 * y + z, rows, :] -= along_z[y][z] + along_y[z][y]

    own = pl.ds(pl.multiple_of(16 * me, 16), 16)

    def send_chunk(k, x0):
        transport(x0)
        for i in range(PAIR):
            cells[x0 + i, own, :] = read[x0 + i, me]
        for off in ORDER:
            to = partner(me, off)
            pltpu.make_async_remote_copy(
                src_ref=read.at[pl.ds(x0, PAIR), to], dst_ref=cells.at[pl.ds(x0, PAIR), own, :],
                send_sem=go_send.at[k], recv_sem=go_recv.at[k],
                device_id=(sp, to), device_id_type=MESH,
            ).start()

    def first_of(k):
        return lax.rem(PAIR * k + 2, layers)

    def inner(k, _):
        send_chunk(k, first_of(k))
        return 0

    lax.fori_loop(0, chunks - 2, inner, 0)

    @pl.when(sp > 0)
    def _():
        to_right.wait_recv()

    @pl.when(sp < spaces - 1)
    def _():
        to_left.wait_recv()

    lax.fori_loop(chunks - 2, chunks, inner, 0)

    def collide(k, _):
        x0 = first_of(k)
        arrived = cells.at[pl.ds(x0, PAIR), pl.ds(0, 240), :]
        pltpu.make_async_copy(arrived, arrived, go_recv.at[k]).wait()
        field = jnp.concatenate([cells[x0], cells[x0 + 1]], 1)
        spec = mul3((lh[...], ll[...]), split(field))
        tc, ts = twiddle[0], twiddle[1]
        parts = []
        for i in range(PAIR):
            re = spec[:FULL, 128 * i:128 * i + 128]
            im = spec[FULL:, 128 * i:128 * i + 128]
            parts.append(jnp.concatenate([re * tc + im * ts, im * tc - re * ts], 1))
        spec = mul3(split(jnp.concatenate(parts, 0)), (rh[...], rl[...]))
        tc, ts = twiddle[0, :HALF, :], twiddle[1, :HALF, :]
        for i in range(PAIR):
            re = spec[FULL * i:FULL * i + HALF, :128].reshape(8, 16, 128)
            im = spec[FULL * i:FULL * i + HALF, 128:].reshape(8, 16, 128)
            re16 = spec[FULL * i + HALF:FULL * (i + 1), :128]
            im16 = spec[FULL * i + HALF:FULL * (i + 1), 128:]
            for t in range(4):
                w = weights[t].reshape(8, 16, 128)
                for r in range(8):
                    w16 = weights16[t, 8 * r:8 * r + 8, :]
                    zr, zi = w[r] * re[r], w[r] * im[r]
                    zr = jnp.concatenate([zr[:8] - w16 * im16[r:r + 1, :], zr[8:]], 0)
                    zi = jnp.concatenate([zi[:8] + w16 * re16[r:r + 1, :], zi[8:]], 0)
                    if t % 2:
                        zr, zi = zi, -zr
                    rows = slice(HALF * (PAIR * t + i) + 16 * r, HALF * (PAIR * t + i) + 16 * r + 16)
                    high, low = split(jnp.concatenate([zr, zi], 1))
                    yh[rows, :] = high
                    yl[rows, :] = low
        fields = []
        for t in range(4):
            rows = slice(PAIR * HALF * t, PAIR * HALF * (t + 1))
            value = mul3((yh[rows, :], yl[rows, :]), (bh[...], bl[...]))
            reals, imags = [], []
            for i in range(PAIR):
                re = value[HALF * i:HALF * (i + 1), :128]
                im = value[HALF * i:HALF * (i + 1), 128:]
                reals.append(re * tc - im * ts)
                imags.append(re * ts + im * tc)
            value = jnp.concatenate([jnp.concatenate(reals, 1), jnp.concatenate(imags, 1)], 0)
            fields.append(mul3((oh[...], ol[...]), split(value)))
        value = fields[0] * fields[2] - fields[1] * fields[3]
        for i in range(PAIR):
            done[x0 + i] = cells[x0 + i] + value[:, 128 * i:128 * i + 128]
        for off in ORDER:
            to = partner(me, off)
            pltpu.make_async_remote_copy(
                src_ref=done.at[pl.ds(x0, PAIR), pl.ds(pl.multiple_of(16 * to, 16), 16), :],
                dst_ref=result.at[pl.ds(x0, PAIR), my_y, my_z],
                send_sem=back_send.at[k], recv_sem=back_recv.at[k],
                device_id=(sp, to), device_id_type=MESH,
            ).start()
        return 0

    lax.fori_loop(0, chunks, collide, 0)

    mine = pltpu.make_async_copy(
        done.at[:, own, :], result.at[:, my_y, my_z], own_sem)
    mine.start()

    def finish(k, _):
        x0 = first_of(k)
        block = cells.at[pl.ds(x0, PAIR), pl.ds(0, 240), :]
        pltpu.make_async_copy(block, block, go_send.at[k]).wait()
        pltpu.make_async_copy(block, block, back_send.at[k]).wait()
        pltpu.make_async_copy(block, block, back_recv.at[k]).wait()
        return 0

    lax.fori_loop(0, chunks, finish, 0)
    mine.wait()

    @pl.when(sp > 0)
    def _():
        to_left.wait_send()

    @pl.when(sp < spaces - 1)
    def _():
        to_right.wait_send()


def place_kernel(source, target, sem):
    copies = []
    for l in range(16):
        copies.append(pltpu.make_async_copy(
            source.at[:, :, :, l, :], target.at[:, :, :, pl.ds(128 * l, 128)], sem.at[l]))
        copies[-1].start()
    for copy in copies:
        copy.wait()


def shards(spaces, dist, cell_kind, inflow, wall_shape, gain_tables, second_tables):
    layers = dist.shape[0]
    mats, twiddle, flips, flip_lane = tables()
    vmem = pl.BlockSpec(memory_space=pltpu.VMEM)
    anywhere = pl.BlockSpec(memory_space=pl.ANY)
    chunks = layers // PAIR
    dma = pltpu.SemaphoreType.DMA
    result = pl.pallas_call(
        functools.partial(step_kernel, spaces, layers),
        out_shape=jax.ShapeDtypeStruct((layers, 4, 4, 16, 128), F32),
        in_specs=[anywhere, pl.BlockSpec(memory_space=pltpu.SMEM)] + [vmem] * 15,
        out_specs=anywhere,
        scratch_shapes=[
            pltpu.VMEM((layers + 4, 4, 4, 16, 128), F32),
            pltpu.VMEM((256, 128), F32),
            pltpu.VMEM((1, 256), F32),
            pltpu.VMEM((16, 1, 256), F32),
            pltpu.VMEM((layers * 16, 128), F32),
            pltpu.VMEM((layers, 16, 16, 128), F32),
            pltpu.VMEM((layers, 256, 128), F32),
            pltpu.VMEM((layers, 256, 128), F32),
            pltpu.VMEM((4, 256, 128), F32),
            pltpu.VMEM((4, HALF, 128), F32),
            pltpu.VMEM((4, 64, 128), F32),
            pltpu.VMEM((4 * PAIR * HALF, 256), BF16),
            pltpu.VMEM((4 * PAIR * HALF, 256), BF16),
            pltpu.VMEM((16, 128), BF16),
            pltpu.VMEM((16, 128), BF16),
            dma((16,)),
            dma((15,)), dma((15,)),
            dma((2,)), dma((2,)),
            dma((chunks,)), dma((chunks,)),
            dma((chunks,)), dma((chunks,)),
            dma,
        ],
        compiler_params=pltpu.CompilerParams(
            collective_id=0, has_side_effects=True, vmem_limit_bytes=32 * 2**20),
    )(
        dist, cell_kind, inflow.reshape(16, 128), wall_shape.reshape(16, 128),
        gain_tables.reshape(256, 128), second_tables.reshape(256, 128),
        *[jnp.asarray(m) for m in mats], jnp.asarray(twiddle), jnp.asarray(flips), jnp.asarray(flip_lane),
    )
    return pl.pallas_call(
        place_kernel,
        out_shape=jax.ShapeDtypeStruct(dist.shape, F32),
        in_specs=[anywhere],
        out_specs=anywhere,
        scratch_shapes=[dma((16,))],
    )(result)


def solution(mesh):
    placed = (P("space", None, None, "vel"), P("space", None, None), P("vel"), P("vel"), P(), P())
    return jax.shard_map(
        functools.partial(shards, mesh.shape["space"]),
        mesh=mesh, in_specs=placed, out_specs=P("space", None, None, "vel"), check_vma=False,
    )
```

time: 685 us -> 129 us (0.19)
  the two profiles are of different devices: /device:TPU:8 before, /device:TPU:1 now
where the time goes in v1:
time: 129 us; the launch traced here: 128 us
  Pallas kernels  112 us (87%)
  local copies, waits for them, and re-layouts  16.6 us (13%)
    pallas_call x1, Pallas kernels, shards(): pl.pallas_call(functools.partial(step_kernel, spaces, layers), out_shape=...  62.9 us
    pallas_call x1, Pallas kernels, shards(): pl.pallas_call(place_kernel, out_shape=jax.ShapeDtypeStruct(dist.shape, F...  48.9 us
    unnamed x35, local copies, waits for them, and re-layouts  16.6 us

profile of v1, /device:TPU:1, one launch (start us, length us, event | category | flops | bytes accessed | tf_op | source)
XLA Modules:
  0.0 128.4 jit_solution(9642776924844749152)
XLA Ops:
  0.0 0.8 copy.18.kind
  0.8 0.0 copy-start.1
  0.8 1.4 %copy-done.1 = f32[12,4,4,2048]{3,2,1,0:T(4,128)S(1)} copy-done((f32[12,4,4,2048]{3,2,1,0:T(4,128)S(1)}, f32[12,4,4,2048]{3,2,1,0:T(4,128)}, u32[]{:S(2)}) %copy-start.1) | copy-done | bytes 1572888
  2.2 0.0 copy-start.2
  2.2 1.0 copy-done.2
  3.3 0.0 copy-start.3
  3.3 0.9 copy-done.3
  4.2 0.0 copy-start.4
  4.2 0.9 copy-done.4
  5.1 0.0 copy-start.5
  5.1 0.9 copy-done.5
  6.0 0.9 copy-done.6
  6.9 0.0 copy-start.7
  6.9 0.9 copy-done.7
  7.8 0.0 copy-start.8
  7.8 0.9 copy-done.8
  8.7 0.0 copy-start.9
  8.7 0.9 copy-done.9
  9.6 0.0 copy-start.10
  9.6 0.9 copy-done.10
  10.5 0.0 copy-start.11
  10.5 0.9 copy-done.11
  11.4 0.0 copy-start.12
  11.4 0.9 copy-done.12
  12.3 0.9 copy-done.13
  13.2 0.8 copy-done.14
  14.1 0.7 copy-done.15
  14.8 0.7 copy-done.16
  15.4 62.9 %shard_map.163.source = f32[12,4,4,16,128]{4,3,2,1,0:T(8,128)S(1)} custom-call(f32[12,4,4,2048]{3,2,1,0:T(4,128)S(1)} %copy-done.1, s32[12,4,4]{2,1,0:T(4,128)S(1)} %copy.18.kind, f32[16,128]{1,0:T(8,128)S(1)} %bitcast.6, f32[16,128]{1,0:T(8,128)S(1)} %bitcast.7, f32[256,128]{1,0:T(8,128)S(1)} %bitcast.4, f32[256,128]{1,0:T(8,128)S(1)} %bitcast.5, ...), custom_call_target="tpu_custom_call" | custom-call | tf_op jit(solution)/shard_map/pallas_call | solution.py:412
  78.3 0.0 copy-start
  78.3 1.2 copy-done
  79.5 48.9 %shard_map.164 = f32[12,4,4,2048]{3,2,1,0:T(4,128)} custom-call(f32[12,4,4,16,128]{4,3,2,1,0:T(8,128)} %copy-done), custom_call_target="tpu_custom_call" | custom-call | tf_op jit(solution)/shard_map/pallas_call | solution.py:447
  (5 shorter events, 0.0 us)
Async XLA Ops:
  0.8 1.4 %copy-start.1 = (f32[12,4,4,2048]{3,2,1,0:T(4,128)S(1)}, f32[12,4,4,2048]{3,2,1,0:T(4,128)}, u32[]{:S(2)}) copy-start(f32[12,4,4,2048]{3,2,1,0:T(4,128)} %dist.1) | copy-start | bytes 4718596
  2.2 1.0 copy-start.2
  3.3 0.9 copy-start.3
  4.2 0.9 copy-start.4
  5.1 0.9 copy-start.5
  6.0 0.9 copy-start.6
  6.9 0.9 copy-start.7
  7.8 0.9 copy-start.8
  8.7 0.9 copy-start.9
  9.6 0.9 copy-start.10
  10.5 0.9 copy-start.11
  11.4 0.9 copy-start.12
  12.3 0.9 copy-start.13
  13.2 0.8 copy-start.14
  14.1 0.7 copy-start.15
  14.8 0.7 copy-start.16
  78.3 1.2 copy-start

commit v2 on v1

--- a/solution.py
+++ b/solution.py
@@ -26,19 +26,6 @@
     (1, 0, 0), (0, 1, 0), (0, 3, 1), (1, 2, 0), (1, 1, 0), (1, 3, 1), (0, 2, 0), (1, 0, 1),
     (0, 1, 1), (0, 3, 0), (1, 2, 1), (1, 1, 1), (1, 3, 0), (0, 2, 1), (0, 0, 1),
 )
-
-
-def halves(table):
-    high = jnp.asarray(table, F32).astype(BF16)
-    low = (jnp.asarray(table, F32) - high.astype(F32)).astype(BF16)
-    return high, low
-
-
-def np_halves(table):
-    table = np.asarray(table, np.float32)
-    high = table.astype(BF16)
-    low = (table - high.astype(np.float32)).astype(BF16)
-    return high, low
 
 
 def tables():
@@ -73,10 +60,8 @@
     flip_lane = np.zeros((128, 128), np.float32)
     flip_lane[((-b_lo) % 4) * 32 + (-c) % 32, lane] = 1
     flips = np.concatenate([flip0, flip1], 0)
-    mats = []
-    for table in (left, right, back, out):
-        mats += list(np_halves(table))
-    return mats, twiddle.astype(np.float32), flips, flip_lane
+    small = np.concatenate([twiddle.reshape(2 * FULL, 128), flip_lane], 0)
+    return np.concatenate([left, right, back, out], 0).astype(np.float32), flips, small.astype(np.float32)
 
 
 def split(value):
@@ -104,9 +89,10 @@
 
 def step_kernel(
     spaces, layers,
-    dist, kind, inflow, wall, gain, second, lh, ll, rh, rl, bh, bl, oh, ol, twiddle, flips, flip_lane,
+    dist, kind, inflow_hbm, wall_hbm, gain_hbm, second_hbm, mats_hbm, flips_hbm, small_hbm,
     result,
-    ext, lane_sums, mass_row, mass_all, scales, read, cells, done, nat, weights, weights16, yh, yl, vh, vl,
+    raw, inflow, wall, gain, second, mats, high, low, flips, small,
+    ext, lane_sums, mass_row, mass_all, scales, read, cells, done, nat, weights, weights16, yh, yl,
     in_sem, mass_send, mass_recv, halo_send, halo_recv, go_send, go_recv, back_send, back_recv, own_sem,
 ):
     sp = lax.axis_index("space")
@@ -116,12 +102,11 @@
     count = layers * 16
 
     loads = []
-    for l in range(16):
-        loads.append(pltpu.make_async_copy(
-            dist.at[:, :, :, pl.ds(128 * l, 128)],
-            ext.at[pl.ds(2, layers), :, :, l, :],
-            in_sem.at[l],
-        ))
+    for i, (source, target) in enumerate((
+        (dist, raw), (wall_hbm, wall), (gain_hbm, gain), (second_hbm, second), (flips_hbm, flips),
+        (small_hbm, small), (inflow_hbm, inflow), (mats_hbm, mats),
+    )):
+        loads.append(pltpu.make_async_copy(source, target, in_sem.at[i]))
         loads[-1].start()
 
     barrier = pltpu.get_barrier_semaphore()
@@ -130,16 +115,21 @@
     for near in (1, spaces - 1):
         pl.semaphore_signal(barrier, inc=1, device_id=(lax.rem(sp + near, spaces), me), device_id_type=MESH)
 
-    lane_sums[...] = jnp.zeros_like(lane_sums)
-    lane_sums[count:count + 8, :] = jnp.concatenate(
-        [jnp.sum(wall[...], axis=0, keepdims=True), jnp.zeros((7, 128), F32)], 0)
-    for load in loads:
-        load.wait()
+    sub = lax.broadcasted_iota(jnp.int32, (8, 128), 0)
+    loads[1].wait()
+    lane_sums[count:256, :] = jnp.zeros((256 - count, 128), F32)
+    lane_sums[count:count + 1, :] = jnp.sum(wall[...], axis=0, keepdims=True)
+    loads[0].wait()
 
     def sum_layer(x, _):
-        block = ext[2 + x].reshape(16, 2, 8, 128)
-        block = jnp.sum(block[:, 0] + block[:, 1], axis=1)
-        lane_sums[pl.ds(pl.multiple_of(x * 16, 16), 16), :] = block
+        pieces = []
+        for y in range(4):
+            block = raw[pl.ds(pl.multiple_of(256 * x + 64 * y, 64), 64), :].reshape(8, 8, 128)
+            block = jnp.sum(block, axis=0)
+            pieces.append(block + pltpu.roll(block, 4, 0))
+        for i in range(2):
+            lane_sums[pl.ds(pl.multiple_of(16 * x + 8 * i, 8), 8), :] = jnp.where(
+                sub < 4, pieces[2 * i], pieces[2 * i + 1])
         return 0
 
     lax.fori_loop(0, layers, sum_layer, 0)
@@ -157,11 +147,14 @@
         sends[-1].start()
 
     lane = lax.broadcasted_iota(jnp.int32, (16, 128), 1) // 32
-    sub = lax.broadcasted_iota(jnp.int32, (8, 128), 0)
+    for load in loads[2:]:
+        load.wait()
+    flip_lane = small[2 * FULL:, :]
+    high[...], low[...] = split(mats[...])
     lane8 = lax.broadcasted_iota(jnp.int32, (8, 128), 1) // 32
     for t, (table, scale) in enumerate(((gain, 1.0 / NV), (second, COLLISION_AXIS / NV))):
         g = table[...]
-        rev = jnp.dot(g, flip_lane[...], precision=HIGH, preferred_element_type=F32)
+        rev = jnp.dot(g, flip_lane, precision=HIGH, preferred_element_type=F32)
         mask = lax.broadcasted_iota(jnp.int32, (256, 128), 1) < 32
         rev0 = jnp.dot(flips[0:256, :], rev, precision=HIGH, preferred_element_type=F32)
         rev1 = jnp.dot(flips[256:512, :], rev, precision=HIGH, preferred_element_type=F32)
@@ -171,13 +164,13 @@
 
     def order_weights(t, _):
         for r in range(8):
-            high, low = r // 4, r % 4
+            upper, lower = r // 4, r % 4
             value = jnp.zeros((16, 128), F32)
             value16 = jnp.zeros((8, 128), F32)
             for q in range(4):
-                rows = nat[t, pl.ds(2 * q + high, 16, stride=8), :]
-                row16 = jnp.broadcast_to(nat[t, pl.ds(128 + 2 * q + high, 1), :], (8, 128))
-                shift = (32 * (q - low)) % 128
+                rows = nat[t, pl.ds(2 * q + upper, 16, stride=8), :]
+                row16 = jnp.broadcast_to(nat[t, pl.ds(128 + 2 * q + upper, 1), :], (8, 128))
+                shift = (32 * (q - lower)) % 128
                 if shift:
                     rows = pltpu.roll(rows, shift, 1)
                     row16 = pltpu.roll(row16, shift, 1)
@@ -198,11 +191,12 @@
     def boundary_layer(x, _):
         for y in range(4):
             for z in range(4):
-                what = jnp.full((8, 128), kind[x, y, z], jnp.int32)
+                what = jnp.full((8, 128), kind[y, z, x], jnp.int32)
                 scale = jnp.broadcast_to(scales[pl.ds(x * 16 + 4 * y + z, 1), :], (8, 128))
                 for e in range(2):
                     rows = slice(8 * e, 8 * e + 8)
-                    value = jnp.where(what == 1, scale * wall[rows, :], ext[2 + x, y, z, rows, :])
+                    value = raw[pl.ds(256 * x + 64 * y + 32 * e + z, 8, stride=4), :]
+                    value = jnp.where(what == 1, scale * wall[rows, :], value)
                     ext[2 + x, y, z, rows, :] = jnp.where(what == 2, inflow[rows, :], value)
         return 0
 
@@ -309,20 +303,24 @@
 
     lax.fori_loop(chunks - 2, chunks, inner, 0)
 
+    lh, ll = high.at[0:2 * FULL], low.at[0:2 * FULL]
+    (rh, bh, oh), (rl, bl, ol) = (
+        [ref.at[2 * FULL + 256 * i:2 * FULL + 256 * (i + 1)] for i in range(3)] for ref in (high, low))
+
     def collide(k, _):
         x0 = first_of(k)
         arrived = cells.at[pl.ds(x0, PAIR), pl.ds(0, 240), :]
         pltpu.make_async_copy(arrived, arrived, go_recv.at[k]).wait()
         field = jnp.concatenate([cells[x0], cells[x0 + 1]], 1)
         spec = mul3((lh[...], ll[...]), split(field))
-        tc, ts = twiddle[0], twiddle[1]
+        tc, ts = small[0:FULL, :], small[FULL:2 * FULL, :]
         parts = []
         for i in range(PAIR):
             re = spec[:FULL, 128 * i:128 * i + 128]
             im = spec[FULL:, 128 * i:128 * i + 128]
             parts.append(jnp.concatenate([re * tc + im * ts, im * tc - re * ts], 1))
         spec = mul3(split(jnp.concatenate(parts, 0)), (rh[...], rl[...]))
-        tc, ts = twiddle[0, :HALF, :], twiddle[1, :HALF, :]
+        tc, ts = small[0:HALF, :], small[FULL:FULL + HALF, :]
         for i in range(PAIR):
             re = spec[FULL * i:FULL * i + HALF, :128].reshape(8, 16, 128)
             im = spec[FULL * i:FULL * i + HALF, 128:].reshape(8, 16, 128)
@@ -338,9 +336,7 @@
                     if t % 2:
                         zr, zi = zi, -zr
                     rows = slice(HALF * (PAIR * t + i) + 16 * r, HALF * (PAIR * t + i) + 16 * r + 16)
-                    high, low = split(jnp.concatenate([zr, zi], 1))
-                    yh[rows, :] = high
-                    yl[rows, :] = low
+                    yh[rows, :], yl[rows, :] = split(jnp.concatenate([zr, zi], 1))
         fields = []
         for t in range(4):
             rows = slice(PAIR * HALF * t, PAIR * HALF * (t + 1))
@@ -392,29 +388,51 @@
         to_right.wait_send()
 
 
-def place_kernel(source, target, sem):
-    copies = []
-    for l in range(16):
-        copies.append(pltpu.make_async_copy(
-            source.at[:, :, :, l, :], target.at[:, :, :, pl.ds(128 * l, 128)], sem.at[l]))
-        copies[-1].start()
-    for copy in copies:
-        copy.wait()
+def place_kernel(layers, source, target, held, rows, in_sem, out_sem):
+    step = layers // 4
+
+    def load(i):
+        return pltpu.make_async_copy(source.at[pl.ds(step * i, step)], held.at[pl.ds(step * i, step)], in_sem.at[i])
+
+    def store(i):
+        part = pl.ds(256 * step * i, 256 * step)
+        return pltpu.make_async_copy(rows.at[part], target.at[part], out_sem.at[i])
+
+    for i in range(4):
+        load(i).start()
+    for i in range(4):
+        load(i).wait()
+
+        def place(x, _):
+            for y in range(4):
+                for z in range(4):
+                    for e in range(2):
+                        rows[pl.ds(256 * x + 64 * y + 32 * e + z, 8, stride=4), :] = held[x, y, z, 8 * e:8 * e + 8, :]
+            return 0
+
+        lax.fori_loop(step * i, step * (i + 1), place, 0)
+        store(i).start()
+    for i in range(4):
+        store(i).wait()
 
 
 def shards(spaces, dist, cell_kind, inflow, wall_shape, gain_tables, second_tables):
     layers = dist.shape[0]
-    mats, twiddle, flips, flip_lane = tables()
-    vmem = pl.BlockSpec(memory_space=pltpu.VMEM)
+    mats, flips, small = tables()
+    rows = dist.reshape(layers, 4, 4, 16, 128).transpose(0, 1, 3, 2, 4).reshape(layers * 256, 128)
     anywhere = pl.BlockSpec(memory_space=pl.ANY)
     chunks = layers // PAIR
     dma = pltpu.SemaphoreType.DMA
     result = pl.pallas_call(
         functools.partial(step_kernel, spaces, layers),
         out_shape=jax.ShapeDtypeStruct((layers, 4, 4, 16, 128), F32),
-        in_specs=[anywhere, pl.BlockSpec(memory_space=pltpu.SMEM)] + [vmem] * 15,
+        in_specs=[anywhere, pl.BlockSpec(memory_space=pltpu.SMEM)] + [anywhere] * 7,
         out_specs=anywhere,
         scratch_shapes=[
+            pltpu.VMEM((layers * 256, 128), F32),
+            pltpu.VMEM((16, 128), F32), pltpu.VMEM((16, 128), F32),
+            pltpu.VMEM((256, 128), F32), pltpu.VMEM((256, 128), F32),
+            pltpu.VMEM(mats.shape, F32), pltpu.VMEM(mats.shape, BF16), pltpu.VMEM(mats.shape, BF16), pltpu.VMEM(flips.shape, F32), pltpu.VMEM(small.shape, F32),
             pltpu.VMEM((layers + 4, 4, 4, 16, 128), F32),
             pltpu.VMEM((256, 128), F32),
             pltpu.VMEM((1, 256), F32),
@@ -428,9 +446,7 @@
             pltpu.VMEM((4, 64, 128), F32),
             pltpu.VMEM((4 * PAIR * HALF, 256), BF16),
             pltpu.VMEM((4 * PAIR * HALF, 256), BF16),
-            pltpu.VMEM((16, 128), BF16),
-            pltpu.VMEM((16, 128), BF16),
-            dma((16,)),
+            dma((8,)),
             dma((15,)), dma((15,)),
             dma((2,)), dma((2,)),
             dma((chunks,)), dma((chunks,)),
@@ -438,19 +454,22 @@
             dma,
         ],
         compiler_params=pltpu.CompilerParams(
-            collective_id=0, has_side_effects=True, vmem_limit_bytes=32 * 2**20),
+            collective_id=0, has_side_effects=True, vmem_limit_bytes=56 * 2**20),
     )(
-        dist, cell_kind, inflow.reshape(16, 128), wall_shape.reshape(16, 128),
+        rows, cell_kind.transpose(1, 2, 0), inflow.reshape(16, 128), wall_shape.reshape(16, 128),
         gain_tables.reshape(256, 128), second_tables.reshape(256, 128),
-        *[jnp.asarray(m) for m in mats], jnp.asarray(twiddle), jnp.asarray(flips), jnp.asarray(flip_lane),
+        jnp.asarray(mats), jnp.asarray(flips), jnp.asarray(small),
     )
-    return pl.pallas_call(
-        place_kernel,
-        out_shape=jax.ShapeDtypeStruct(dist.shape, F32),
+    placed = pl.pallas_call(
+        functools.partial(place_kernel, layers),
+        out_shape=jax.ShapeDtypeStruct((layers * 256, 128), F32),
         in_specs=[anywhere],
         out_specs=anywhere,
-        scratch_shapes=[dma((16,))],
+        scratch_shapes=[
+            pltpu.VMEM((layers, 4, 4, 16, 128), F32), pltpu.VMEM((layers * 256, 128), F32), dma((4,)), dma((4,))],
+        compiler_params=pltpu.CompilerParams(vmem_limit_bytes=56 * 2**20),
     )(result)
+    return placed.reshape(layers, 4, 16, 4, 128).transpose(0, 1, 3, 2, 4).reshape(dist.shape)
 
 
 def solution(mesh):

time: 129 us -> 64.2 us (0.50)
  Pallas kernels: 112 us -> 64.1 us
  local copies, waits for them, and re-layouts: 16.6 us -> 0 us
    pallas_call x1, Pallas kernels: 48.9 us -> 2.23 us  [shards(): pl.pallas_call(functools.partial(place_kernel, layers), out_shape=jax.Sha...]
    unnamed x35 -> x0, local copies, waits for them, and re-layouts: 16.6 us -> none
where the time goes in v2:
time: 64.2 us; the launch traced here: 64.1 us
  Pallas kernels  64.1 us (100%)
    pallas_call x1, Pallas kernels, shards(): pl.pallas_call(functools.partial(step_kernel, spaces, layers), out_shape=...  61.8 us
    pallas_call x1, Pallas kernels, shards(): pl.pallas_call(functools.partial(place_kernel, layers), out_shape=jax.Sha...  2.23 us

profile of v2, /device:TPU:1, one launch (start us, length us, event | category | flops | bytes accessed | tf_op | source)
XLA Modules:
  0.0 64.1 jit_solution(8354890581206816580)
XLA Ops:
  0.0 61.8 %shard_map.91.source = f32[12,4,4,16,128]{4,3,2,1,0:T(8,128)} custom-call(f32[3072,128]{1,0:T(8,128)} %bitcast.15, s32[4,4,12]{2,1,0:T(4,128)} %bitcast.18, f32[16,128]{1,0:T(8,128)} %bitcast.19, f32[16,128]{1,0:T(8,128)} %bitcast.20, f32[256,128]{1,0:T(8,128)} %bitcast.16, f32[256,128]{1,0:T(8,128)} %bitcast.17, f32[1040,256]{1,0:T(8,128)} %constant.6.clone.mats_hbm, ...), custom_call_target="tpu_custom_call" | custom-call | tf_op jit(solution)/shard_map/pallas_call | solution.py:426
  61.9 2.2 %shard_map.92 = f32[3072,128]{1,0:T(8,128)} custom-call(f32[12,4,4,16,128]{4,3,2,1,0:T(8,128)} %shard_map.91.source), custom_call_target="tpu_custom_call" | custom-call | tf_op jit(solution)/shard_map/pallas_call | solution.py:463

commit v3 on v2

--- a/solution.py
+++ b/solution.py
@@ -93,13 +93,14 @@
     result,
     raw, inflow, wall, gain, second, mats, high, low, flips, small,
     ext, lane_sums, mass_row, mass_all, scales, read, cells, done, nat, weights, weights16, yh, yl,
-    in_sem, mass_send, mass_recv, halo_send, halo_recv, go_send, go_recv, back_send, back_recv, own_sem,
+    relay, in_sem, relay_sem, mass_send, mass_recv, halo_send, halo_recv, go_send, go_recv, back_send, back_recv, own_sem,
 ):
     sp = lax.axis_index("space")
     me = lax.axis_index("vel")
     my_y, my_z = me // 4, me % 4
     chunks = layers // PAIR
     count = layers * 16
+    cross = spaces // 2
 
     loads = []
     for i, (source, target) in enumerate((
@@ -112,8 +113,16 @@
     barrier = pltpu.get_barrier_semaphore()
     for off in ORDER:
         pl.semaphore_signal(barrier, inc=1, device_id=(sp, partner(me, off)), device_id_type=MESH)
-    for near in (1, spaces - 1):
-        pl.semaphore_signal(barrier, inc=1, device_id=(lax.rem(sp + near, spaces), me), device_id_type=MESH)
+    greeted = 0
+    for other in range(spaces):
+        ends = other in (cross - 1, cross)
+        near = (sp == other - 1) | (sp == other + 1) | (sp == cross - 1) | (sp == cross)
+        greet = (sp != other) if ends else near & (sp != other)
+        greeted = greeted + jnp.where(greet, 1, 0)
+
+        @pl.when(greet)
+        def _():
+            pl.semaphore_signal(barrier, inc=1, device_id=(other, me), device_id_type=MESH)
 
     sub = lax.broadcasted_iota(jnp.int32, (8, 128), 0)
     loads[1].wait()
@@ -136,7 +145,7 @@
     mass_row[...] = jnp.sum(lane_sums[...].T, axis=0, keepdims=True)
     mass_all[me] = mass_row[...]
 
-    pl.semaphore_wait(barrier, len(ORDER) + 2)
+    pl.semaphore_wait(barrier, len(ORDER) + greeted)
 
     sends = []
     for i, off in enumerate(ORDER):
@@ -183,7 +192,7 @@
     lax.fori_loop(0, 4, order_weights, 0)
 
     for copy in sends:
-        copy.wait()
+        copy.wait_recv()
     total = jnp.sum(mass_all[...], axis=0)
     totals = jnp.broadcast_to(total, (128, 256)).T
     scales[...] = totals[:count] / totals[count:count + 1]
@@ -211,13 +220,40 @@
         send_sem=halo_send.at[1], recv_sem=halo_recv.at[1],
         device_id=(lax.rem(sp + 1, spaces), me), device_id_type=MESH)
 
-    @pl.when(sp > 0)
+    def piece(x, p):
+        return ext.at[pl.ds(x, 2), p // 2, pl.ds(2 * (p % 2), 2)]
+
+    @pl.when((sp > 0) & (sp != cross))
     def _():
         to_left.start()
 
-    @pl.when(sp < spaces - 1)
+    @pl.when((sp < spaces - 1) & (sp != cross - 1))
     def _():
         to_right.start()
+
+    @pl.when(sp == cross - 1)
+    def _():
+        for p in range(cross):
+            pltpu.make_async_remote_copy(
+                src_ref=piece(layers, p), dst_ref=piece(0, p) if p == 0 else relay,
+                send_sem=halo_send.at[1], recv_sem=halo_recv.at[1] if p == 0 else relay_sem.at[0],
+                device_id=(cross + p, me), device_id_type=MESH).start()
+
+    @pl.when(sp == cross)
+    def _():
+        for p in range(cross):
+            pltpu.make_async_remote_copy(
+                src_ref=piece(2, p), dst_ref=piece(layers + 2, p) if p == cross - 1 else relay,
+                send_sem=halo_send.at[0], recv_sem=halo_recv.at[0] if p == cross - 1 else relay_sem.at[0],
+                device_id=(p, me), device_id_type=MESH).start()
+
+    up = lax.rem(sp, cross)
+    relay_right = pltpu.make_async_remote_copy(
+        src_ref=relay, dst_ref=piece(0, up), send_sem=relay_sem.at[1], recv_sem=halo_recv.at[1],
+        device_id=(cross, me), device_id_type=MESH)
+    relay_left = pltpu.make_async_remote_copy(
+        src_ref=relay, dst_ref=piece(layers + 2, up), send_sem=relay_sem.at[1], recv_sem=halo_recv.at[0],
+        device_id=(cross - 1, me), device_id_type=MESH)
 
     @pl.when(sp == 0)
     def _():
@@ -291,7 +327,19 @@
         send_chunk(k, first_of(k))
         return 0
 
-    lax.fori_loop(0, chunks - 2, inner, 0)
+    lax.fori_loop(0, 2, inner, 0)
+
+    @pl.when(sp > cross)
+    def _():
+        pltpu.make_async_copy(relay, relay, relay_sem.at[0]).wait()
+        relay_right.start()
+
+    @pl.when(sp < cross - 1)
+    def _():
+        pltpu.make_async_copy(relay, relay, relay_sem.at[0]).wait()
+        relay_left.start()
+
+    lax.fori_loop(2, chunks - 2, inner, 0)
 
     @pl.when(sp > 0)
     def _():
@@ -387,6 +435,17 @@
     def _():
         to_right.wait_send()
 
+    @pl.when(sp > cross)
+    def _():
+        relay_right.wait_send()
+
+    @pl.when(sp < cross - 1)
+    def _():
+        relay_left.wait_send()
+
+    for copy in sends:
+        copy.wait_send()
+
 
 def place_kernel(layers, source, target, held, rows, in_sem, out_sem):
     step = layers // 4
@@ -446,7 +505,8 @@
             pltpu.VMEM((4, 64, 128), F32),
             pltpu.VMEM((4 * PAIR * HALF, 256), BF16),
             pltpu.VMEM((4 * PAIR * HALF, 256), BF16),
-            dma((8,)),
+            pltpu.VMEM((2, 2, 16, 128), F32),
+            dma((8,)), dma((2,)),
             dma((15,)), dma((15,)),
             dma((2,)), dma((2,)),
             dma((chunks,)), dma((chunks,)),

time: 64.2 us -> 58.2 us (0.907)
  the two profiles are of different devices: /device:TPU:1 before, /device:TPU:9 now
where the time goes in v3:
time: 58.2 us; the launch traced here: 58.1 us
  Pallas kernels  58.1 us (100%)
    pallas_call x1, Pallas kernels, shards(): pl.pallas_call(functools.partial(step_kernel, spaces, layers), out_shape=...  55.9 us
    pallas_call x1, Pallas kernels, shards(): pl.pallas_call(functools.partial(place_kernel, layers), out_shape=jax.Sha...  2.23 us

profile of v3, /device:TPU:9, one launch (start us, length us, event | category | flops | bytes accessed | tf_op | source)
XLA Modules:
  0.0 58.1 jit_solution(9416026386272530674)
XLA Ops:
  0.0 55.9 %shard_map.91.source = f32[12,4,4,16,128]{4,3,2,1,0:T(8,128)} custom-call(f32[3072,128]{1,0:T(8,128)} %bitcast.15, s32[4,4,12]{2,1,0:T(4,128)} %bitcast.18, f32[16,128]{1,0:T(8,128)} %bitcast.19, f32[16,128]{1,0:T(8,128)} %bitcast.20, f32[256,128]{1,0:T(8,128)} %bitcast.16, f32[256,128]{1,0:T(8,128)} %bitcast.17, f32[1040,256]{1,0:T(8,128)} %constant.6.clone.mats_hbm, ...), custom_call_target="tpu_custom_call" | custom-call | tf_op jit(solution)/shard_map/pallas_call | solution.py:485
  55.9 2.2 %shard_map.92 = f32[3072,128]{1,0:T(8,128)} custom-call(f32[12,4,4,16,128]{4,3,2,1,0:T(8,128)} %shard_map.91.source), custom_call_target="tpu_custom_call" | custom-call | tf_op jit(solution)/shard_map/pallas_call | solution.py:523

commit v4 on v3

--- a/solution.py
+++ b/solution.py
@@ -105,7 +105,7 @@
     loads = []
     for i, (source, target) in enumerate((
         (dist, raw), (wall_hbm, wall), (gain_hbm, gain), (second_hbm, second), (flips_hbm, flips),
-        (small_hbm, small), (inflow_hbm, inflow), (mats_hbm, mats),
+        (small_hbm, small), (mats_hbm, mats), (inflow_hbm, inflow),
     )):
         loads.append(pltpu.make_async_copy(source, target, in_sem.at[i]))
         loads[-1].start()
@@ -156,41 +156,44 @@
         sends[-1].start()
 
     lane = lax.broadcasted_iota(jnp.int32, (16, 128), 1) // 32
-    for load in loads[2:]:
-        load.wait()
-    flip_lane = small[2 * FULL:, :]
-    high[...], low[...] = split(mats[...])
     lane8 = lax.broadcasted_iota(jnp.int32, (8, 128), 1) // 32
-    for t, (table, scale) in enumerate(((gain, 1.0 / NV), (second, COLLISION_AXIS / NV))):
-        g = table[...]
-        rev = jnp.dot(g, flip_lane, precision=HIGH, preferred_element_type=F32)
-        mask = lax.broadcasted_iota(jnp.int32, (256, 128), 1) < 32
-        rev0 = jnp.dot(flips[0:256, :], rev, precision=HIGH, preferred_element_type=F32)
-        rev1 = jnp.dot(flips[256:512, :], rev, precision=HIGH, preferred_element_type=F32)
-        rev = jnp.where(mask, rev0, rev1)
-        nat[2 * t] = (0.5 * scale) * (g + rev)
-        nat[2 * t + 1] = (0.5 * scale) * (g - rev)
-
-    def order_weights(t, _):
-        for r in range(8):
-            upper, lower = r // 4, r % 4
-            value = jnp.zeros((16, 128), F32)
-            value16 = jnp.zeros((8, 128), F32)
-            for q in range(4):
-                rows = nat[t, pl.ds(2 * q + upper, 16, stride=8), :]
-                row16 = jnp.broadcast_to(nat[t, pl.ds(128 + 2 * q + upper, 1), :], (8, 128))
-                shift = (32 * (q - lower)) % 128
-                if shift:
-                    rows = pltpu.roll(rows, shift, 1)
-                    row16 = pltpu.roll(row16, shift, 1)
-                value = jnp.where(lane == q, rows, value)
-                value16 = jnp.where(lane8 == q, row16, value16)
-            weights[t, 16 * r:16 * r + 16, :] = value
-            weights16[t, 8 * r:8 * r + 8, :] = jnp.where(sub == 0, value16, 0.0)
-        return 0
-
-    lax.fori_loop(0, 4, order_weights, 0)
-
+
+    def prepare():
+        for load in loads[2:-1]:
+            load.wait()
+        flip_lane = small[2 * FULL:, :]
+        high[...], low[...] = split(mats[...])
+        for t, (table, scale) in enumerate(((gain, 1.0 / NV), (second, COLLISION_AXIS / NV))):
+            g = table[...]
+            rev = jnp.dot(g, flip_lane, precision=HIGH, preferred_element_type=F32)
+            mask = lax.broadcasted_iota(jnp.int32, (256, 128), 1) < 32
+            rev0 = jnp.dot(flips[0:256, :], rev, precision=HIGH, preferred_element_type=F32)
+            rev1 = jnp.dot(flips[256:512, :], rev, precision=HIGH, preferred_element_type=F32)
+            rev = jnp.where(mask, rev0, rev1)
+            nat[2 * t] = (0.5 * scale) * (g + rev)
+            nat[2 * t + 1] = (0.5 * scale) * (g - rev)
+
+        def order_weights(t, _):
+            for r in range(8):
+                upper, lower = r // 4, r % 4
+                value = jnp.zeros((16, 128), F32)
+                value16 = jnp.zeros((8, 128), F32)
+                for q in range(4):
+                    rows = nat[t, pl.ds(2 * q + upper, 16, stride=8), :]
+                    row16 = jnp.broadcast_to(nat[t, pl.ds(128 + 2 * q + upper, 1), :], (8, 128))
+                    shift = (32 * (q - lower)) % 128
+                    if shift:
+                        rows = pltpu.roll(rows, shift, 1)
+                        row16 = pltpu.roll(row16, shift, 1)
+                    value = jnp.where(lane == q, rows, value)
+                    value16 = jnp.where(lane8 == q, row16, value16)
+                weights[t, 16 * r:16 * r + 16, :] = value
+                weights16[t, 8 * r:8 * r + 8, :] = jnp.where(sub == 0, value16, 0.0)
+            return 0
+
+        lax.fori_loop(0, 4, order_weights, 0)
+
+    loads[-1].wait()
     for copy in sends:
         copy.wait_recv()
     total = jnp.sum(mass_all[...], axis=0)
@@ -209,8 +212,6 @@
                     ext[2 + x, y, z, rows, :] = jnp.where(what == 2, inflow[rows, :], value)
         return 0
 
-    lax.fori_loop(0, 2, boundary_layer, 0)
-    lax.fori_loop(layers - 2, layers, boundary_layer, 0)
     to_left = pltpu.make_async_remote_copy(
         src_ref=ext.at[pl.ds(2, 2)], dst_ref=ext.at[pl.ds(layers + 2, 2)],
         send_sem=halo_send.at[0], recv_sem=halo_recv.at[0],
@@ -223,30 +224,6 @@
     def piece(x, p):
         return ext.at[pl.ds(x, 2), p // 2, pl.ds(2 * (p % 2), 2)]
 
-    @pl.when((sp > 0) & (sp != cross))
-    def _():
-        to_left.start()
-
-    @pl.when((sp < spaces - 1) & (sp != cross - 1))
-    def _():
-        to_right.start()
-
-    @pl.when(sp == cross - 1)
-    def _():
-        for p in range(cross):
-            pltpu.make_async_remote_copy(
-                src_ref=piece(layers, p), dst_ref=piece(0, p) if p == 0 else relay,
-                send_sem=halo_send.at[1], recv_sem=halo_recv.at[1] if p == 0 else relay_sem.at[0],
-                device_id=(cross + p, me), device_id_type=MESH).start()
-
-    @pl.when(sp == cross)
-    def _():
-        for p in range(cross):
-            pltpu.make_async_remote_copy(
-                src_ref=piece(2, p), dst_ref=piece(layers + 2, p) if p == cross - 1 else relay,
-                send_sem=halo_send.at[0], recv_sem=halo_recv.at[0] if p == cross - 1 else relay_sem.at[0],
-                device_id=(p, me), device_id_type=MESH).start()
-
     up = lax.rem(sp, cross)
     relay_right = pltpu.make_async_remote_copy(
         src_ref=relay, dst_ref=piece(0, up), send_sem=relay_sem.at[1], recv_sem=halo_recv.at[1],
@@ -263,7 +240,6 @@
     def _():
         ext[layers + 2:layers + 4] = jnp.zeros((2, 4, 4, 16, 128), F32)
 
-    lax.fori_loop(2, layers - 2, boundary_layer, 0)
 
     b_index = 4 * lax.broadcasted_iota(jnp.int32, (8, 128), 0) + lane8
     c_index = lax.broadcasted_iota(jnp.int32, (8, 128), 1) % 32
@@ -321,35 +297,38 @@
             ).start()
 
     def first_of(k):
-        return lax.rem(PAIR * k + 2, layers)
+        return (PAIR * k + 2) % layers
 
     def inner(k, _):
         send_chunk(k, first_of(k))
         return 0
 
-    lax.fori_loop(0, 2, inner, 0)
-
-    @pl.when(sp > cross)
-    def _():
-        pltpu.make_async_copy(relay, relay, relay_sem.at[0]).wait()
-        relay_right.start()
-
-    @pl.when(sp < cross - 1)
-    def _():
-        pltpu.make_async_copy(relay, relay, relay_sem.at[0]).wait()
-        relay_left.start()
-
-    lax.fori_loop(2, chunks - 2, inner, 0)
-
-    @pl.when(sp > 0)
-    def _():
-        to_right.wait_recv()
-
-    @pl.when(sp < spaces - 1)
-    def _():
-        to_left.wait_recv()
-
-    lax.fori_loop(chunks - 2, chunks, inner, 0)
+    lax.fori_loop(0, 2, boundary_layer, 0)
+    lax.fori_loop(layers - 2, layers, boundary_layer, 0)
+
+    @pl.when((sp > 0) & (sp != cross))
+    def _():
+        to_left.start()
+
+    @pl.when((sp < spaces - 1) & (sp != cross - 1))
+    def _():
+        to_right.start()
+
+    @pl.when(sp == cross - 1)
+    def _():
+        for p in range(cross):
+            pltpu.make_async_remote_copy(
+                src_ref=piece(layers, p), dst_ref=piece(0, p) if p == 0 else relay,
+                send_sem=halo_send.at[1], recv_sem=halo_recv.at[1] if p == 0 else relay_sem.at[0],
+                device_id=(cross + p, me), device_id_type=MESH).start()
+
+    @pl.when(sp == cross)
+    def _():
+        for p in range(cross):
+            pltpu.make_async_remote_copy(
+                src_ref=piece(2, p), dst_ref=piece(layers + 2, p) if p == cross - 1 else relay,
+                send_sem=halo_send.at[0], recv_sem=halo_recv.at[0] if p == cross - 1 else relay_sem.at[0],
+                device_id=(p, me), device_id_type=MESH).start()
 
     lh, ll = high.at[0:2 * FULL], low.at[0:2 * FULL]
     (rh, bh, oh), (rl, bl, ol) = (
@@ -410,7 +389,40 @@
             ).start()
         return 0
 
-    lax.fori_loop(0, chunks, collide, 0)
+    lax.fori_loop(2, 6, boundary_layer, 0)
+    send_chunk(0, first_of(0))
+
+    def bounded(k, _):
+        lax.fori_loop(2 * k + 4, 2 * k + 6, boundary_layer, 0)
+        return inner(k, 0)
+
+    lax.fori_loop(1, chunks - 3, bounded, 0)
+
+    @pl.when(sp > cross)
+    def _():
+        pltpu.make_async_copy(relay, relay, relay_sem.at[0]).wait()
+        relay_right.start()
+
+    @pl.when(sp < cross - 1)
+    def _():
+        pltpu.make_async_copy(relay, relay, relay_sem.at[0]).wait()
+        relay_left.start()
+
+    inner(chunks - 3, 0)
+    prepare()
+    lax.fori_loop(0, 1, collide, 0)
+
+    @pl.when(sp > 0)
+    def _():
+        to_right.wait_recv()
+
+    @pl.when(sp < spaces - 1)
+    def _():
+        to_left.wait_recv()
+
+    lax.fori_loop(chunks - 2, chunks, inner, 0)
+
+    lax.fori_loop(1, chunks, collide, 0)
 
     mine = pltpu.make_async_copy(
         done.at[:, own, :], result.at[:, my_y, my_z], own_sem)

time: 58.2 us -> 57 us (0.979)
  the two profiles are of different devices: /device:TPU:9 before, /device:TPU:129 now
where the time goes in v4:
time: 57 us; the launch traced here: 56.8 us
  Pallas kernels  56.8 us (100%)
    pallas_call x1, Pallas kernels, shards(): pl.pallas_call(functools.partial(step_kernel, spaces, layers), out_shape=...  54.6 us
    pallas_call x1, Pallas kernels, shards(): pl.pallas_call(functools.partial(place_kernel, layers), out_shape=jax.Sha...  2.23 us

profile of v4, /device:TPU:129, one launch (start us, length us, event | category | flops | bytes accessed | tf_op | source)
XLA Modules:
  0.0 56.8 jit_solution(15921991351787280301)
XLA Ops:
  0.0 54.6 %shard_map.91.source = f32[12,4,4,16,128]{4,3,2,1,0:T(8,128)} custom-call(f32[3072,128]{1,0:T(8,128)} %bitcast.15, s32[4,4,12]{2,1,0:T(4,128)} %bitcast.18, f32[16,128]{1,0:T(8,128)} %bitcast.19, f32[16,128]{1,0:T(8,128)} %bitcast.20, f32[256,128]{1,0:T(8,128)} %bitcast.16, f32[256,128]{1,0:T(8,128)} %bitcast.17, f32[1040,256]{1,0:T(8,128)} %constant.6.clone.mats_hbm, ...), custom_call_target="tpu_custom_call" | custom-call | tf_op jit(solution)/shard_map/pallas_call | solution.py:497
  54.6 2.2 %shard_map.92 = f32[3072,128]{1,0:T(8,128)} custom-call(f32[12,4,4,16,128]{4,3,2,1,0:T(8,128)} %shard_map.91.source), custom_call_target="tpu_custom_call" | custom-call | tf_op jit(solution)/shard_map/pallas_call | solution.py:535

commit v5 on v4

--- a/solution.py
+++ b/solution.py
@@ -23,8 +23,8 @@
 PAIR = 2
 
 ORDER = (
-    (1, 0, 0), (0, 1, 0), (0, 3, 1), (1, 2, 0), (1, 1, 0), (1, 3, 1), (0, 2, 0), (1, 0, 1),
-    (0, 1, 1), (0, 3, 0), (1, 2, 1), (1, 1, 1), (1, 3, 0), (0, 2, 1), (0, 0, 1),
+    (1, 2, 0), (1, 2, 1), (1, 1, 0), (1, 3, 0), (1, 1, 1), (1, 3, 1), (1, 0, 0), (0, 2, 0),
+    (1, 0, 1), (0, 2, 1), (0, 1, 0), (0, 3, 0), (0, 1, 1), (0, 3, 1), (0, 0, 1),
 )
 
 
@@ -193,6 +193,7 @@
 
         lax.fori_loop(0, 4, order_weights, 0)
 
+    prepare()
     loads[-1].wait()
     for copy in sends:
         copy.wait_recv()
@@ -409,7 +410,6 @@
         relay_left.start()
 
     inner(chunks - 3, 0)
-    prepare()
     lax.fori_loop(0, 1, collide, 0)
 
     @pl.when(sp > 0)

time: 57 us -> 55.4 us (0.972)
  the two profiles are of different devices: /device:TPU:129 before, /device:TPU:1 now
where the time goes in v5:
time: 55.4 us; the launch traced here: 54.7 us
  Pallas kernels  54.7 us (99%)
    pallas_call x1, Pallas kernels, shards(): pl.pallas_call(functools.partial(step_kernel, spaces, layers), out_shape=...  52.5 us
    pallas_call x1, Pallas kernels, shards(): pl.pallas_call(functools.partial(place_kernel, layers), out_shape=jax.Sha...  2.23 us

profile of v5, /device:TPU:1, one launch (start us, length us, event | category | flops | bytes accessed | tf_op | source)
XLA Modules:
  0.0 54.7 jit_solution(16625001266192594718)
XLA Ops:
  0.0 52.5 %shard_map.91.source = f32[12,4,4,16,128]{4,3,2,1,0:T(8,128)} custom-call(f32[3072,128]{1,0:T(8,128)} %bitcast.15, s32[4,4,12]{2,1,0:T(4,128)} %bitcast.18, f32[16,128]{1,0:T(8,128)} %bitcast.19, f32[16,128]{1,0:T(8,128)} %bitcast.20, f32[256,128]{1,0:T(8,128)} %bitcast.16, f32[256,128]{1,0:T(8,128)} %bitcast.17, f32[1040,256]{1,0:T(8,128)} %constant.6.clone.mats_hbm, ...), custom_call_target="tpu_custom_call" | custom-call | tf_op jit(solution)/shard_map/pallas_call | solution.py:497
  52.5 2.2 %shard_map.92 = f32[3072,128]{1,0:T(8,128)} custom-call(f32[12,4,4,16,128]{4,3,2,1,0:T(8,128)} %shard_map.91.source), custom_call_target="tpu_custom_call" | custom-call | tf_op jit(solution)/shard_map/pallas_call | solution.py:535

commit v6 on v5

--- a/solution.py
+++ b/solution.py
@@ -399,6 +399,8 @@
 
     lax.fori_loop(1, chunks - 3, bounded, 0)
 
+    inner(chunks - 3, 0)
+
     @pl.when(sp > cross)
     def _():
         pltpu.make_async_copy(relay, relay, relay_sem.at[0]).wait()
@@ -409,7 +411,6 @@
         pltpu.make_async_copy(relay, relay, relay_sem.at[0]).wait()
         relay_left.start()
 
-    inner(chunks - 3, 0)
     lax.fori_loop(0, 1, collide, 0)
 
     @pl.when(sp > 0)

time: 55.4 us -> 55.1 us (level)
  no operation moved by 1% of the time
where the time goes in v6:
time: 55.1 us; the launch traced here: 54.7 us
  Pallas kernels  54.7 us (99%)
    pallas_call x1, Pallas kernels, shards(): pl.pallas_call(functools.partial(step_kernel, spaces, layers), out_shape=...  52.5 us
    pallas_call x1, Pallas kernels, shards(): pl.pallas_call(functools.partial(place_kernel, layers), out_shape=jax.Sha...  2.23 us

profile of v6, /device:TPU:1, one launch (start us, length us, event | category | flops | bytes accessed | tf_op | source)
XLA Modules:
  0.0 54.7 jit_solution(17632421427332738372)
XLA Ops:
  0.0 52.5 %shard_map.91.source = f32[12,4,4,16,128]{4,3,2,1,0:T(8,128)} custom-call(f32[3072,128]{1,0:T(8,128)} %bitcast.15, s32[4,4,12]{2,1,0:T(4,128)} %bitcast.18, f32[16,128]{1,0:T(8,128)} %bitcast.19, f32[16,128]{1,0:T(8,128)} %bitcast.20, f32[256,128]{1,0:T(8,128)} %bitcast.16, f32[256,128]{1,0:T(8,128)} %bitcast.17, f32[1040,256]{1,0:T(8,128)} %constant.6.clone.mats_hbm, ...), custom_call_target="tpu_custom_call" | custom-call | tf_op jit(solution)/shard_map/pallas_call | solution.py:498
  52.5 2.2 %shard_map.92 = f32[3072,128]{1,0:T(8,128)} custom-call(f32[12,4,4,16,128]{4,3,2,1,0:T(8,128)} %shard_map.91.source), custom_call_target="tpu_custom_call" | custom-call | tf_op jit(solution)/shard_map/pallas_call | solution.py:536
